TPU v7x, 32 devices: a whole 2x2x4 slice. The times are simulated.
32 devices in a mesh: line: 4 (over y, core), tile: 8 (over z, x).
Axes of the slice: x: 2, y: 2, z: 4, core: 2. Of those that a mesh axis runs over, the one named last changes fastest.
Arguments:
- traces: bfloat16 [8, 2048, 128], P('tile', 'line'), may hold values from -6 to 6
- codes: int32 [8, 64], P('tile'), may hold values from 0 to 255
- routes: int32 [4, 128], P('line', 'tile'), may hold values from 0 to 7, as said below
- beam_matrix: bfloat16 [4, 8, 2, 4096, 1024], P('line', 'tile'), may hold values from -0.046875 to 0.046875
- dip_filter: float32 [5, 5], replicated, may hold values from -1 to 1
Outputs:
- migrated: float32 [2, 64, 64, 128], P(None, 'line', 'tile')
Inputs may be any that keep to these rules, and one draw needn't show every extreme that they name: `routes`: entry [l, f * 16 + b] is the depth tile that block b of frequency f on line l goes to. Among the 16 entries of one device no tile appears more than 4 times, and in every line some device names one tile exactly 4 times. Among the entries of one line no tile appears more than 32 times, and in every line one tile appears exactly 32 times.
All inputs are finite; a program needn't handle non-finite values.
Results may differ from a plain program's by a relative error of at most 0.004.
Values may be sent and summed in bfloat16 or wider, within the bound.
A program may use at most 64 MiB of HBM per device.

v0:
```python
import jax
import jax.numpy as jnp
from jax import lax
from jax.sharding import PartitionSpec as P

S = 64
P_SIZE = 256
WIN = 128
BR = 128
TZ = 8
TX = 128
MAXB = 32
SEND_MOST = 4


def passed_along(value, axis, steps):
    count = lax.axis_size(axis)
    first, last = (max(0, -steps), min(count, count - steps))
    return lax.ppermute(value, axis, [(source, source + steps) for source in range(first, last)])


def with_halo(cells, sides, width):
    for axis, dim in sides:
        count = lax.axis_size(axis)
        ends = count - 1
        head = lax.slice_in_dim(cells, 0, width, axis=dim)
        tail = lax.slice_in_dim(cells, cells.shape[dim] - width, cells.shape[dim], axis=dim)
        cells = jnp.concatenate(
            [
                lax.ppermute(tail, axis, [(i, (i + 1) % count) for i in range(ends)]),
                cells,
                lax.ppermute(head, axis, [((i + 1) % count, i) for i in range(ends)]),
            ],
            axis=dim,
        )
    return cells


def slant_table(frequency, freq_count):
    slopes = jnp.arange(P_SIZE, dtype=jnp.float32) - P_SIZE / 2
    offsets = jnp.arange(WIN, dtype=jnp.float32) - (WIN - 1) / 2
    factor = 2.0 + frequency.astype(jnp.float32) / freq_count
    phase_angle = jnp.pi * factor * slopes[:, None] * offsets[None, :] / WIN
    taper_row = jnp.exp(-0.5 * (offsets / (0.4 * WIN)) ** 2)
    taper_row = taper_row / jnp.sqrt(jnp.sum(taper_row * taper_row))
    return jnp.concatenate(
        [taper_row * jnp.cos(phase_angle), -taper_row * jnp.sin(phase_angle)], 0
    ).astype(jnp.bfloat16)


def rotate(stacked, code_row):
    real_part = stacked[..., :P_SIZE, :S] - stacked[..., P_SIZE:, S:]
    imag_part = stacked[..., :P_SIZE, S:] + stacked[..., P_SIZE:, :S]
    code_angle = 2.0 * jnp.pi * code_row.astype(jnp.float32) / 256.0
    cosine = jnp.cos(code_angle)
    sine_part = jnp.sin(code_angle)
    return jnp.concatenate(
        [real_part * cosine + imag_part * sine_part, imag_part * cosine - real_part * sine_part], -1
    ).astype(jnp.bfloat16)


def dip_apply(padded, dip_filter):
    depth_rows = padded.shape[2] - 4
    widened = jnp.pad(padded, ((0, 0), (0, 0), (0, 0), (2, 2)))
    result = jnp.zeros(padded.shape[:2] + (depth_rows, TX), jnp.float32)
    for down_step in range(5):
        for side_step in range(5):
            result = (
                result
                + dip_filter[down_step, side_step]
                * widened[:, :, down_step : down_step + depth_rows, side_step : side_step + TX]
            )
    return result


def per_device(traces, codes, routes, beam_matrix, dip_filter):
    tile_count = lax.axis_size("tile")
    my_tile = lax.axis_index("tile")
    half_win = WIN // 2
    row_width = BR * 2 * S
    local_traces = traces[0]
    next_rim = passed_along(local_traces[:half_win], "line", -1)
    extended = jnp.concatenate([local_traces, next_rim], 0)
    halves = extended.reshape(-1, half_win, 2 * S)
    windows = jnp.concatenate([halves[:-1], halves[1:]], 1)
    table_now = slant_table(my_tile, tile_count)
    stacked = jnp.einsum("pj,wjc->wpc", table_now, windows, preferred_element_type=jnp.float32)
    beam_rows = rotate(stacked, codes[0])
    blocks = beam_rows.reshape(-1, row_width)
    route_row = routes[0]
    peer_ids = jnp.arange(tile_count)
    member = (route_row[:, None] == peer_ids[None, :]).astype(jnp.int32)
    before = jnp.cumsum(member, 0) - member
    rank_in = jnp.sum(before * member, 1)
    send_slot = route_row * SEND_MOST + rank_in
    picker = (jnp.arange(tile_count * SEND_MOST)[:, None] == send_slot[None, :]).astype(
        jnp.bfloat16
    )
    outgoing = jnp.dot(picker, blocks, preferred_element_type=jnp.float32).astype(jnp.bfloat16)
    outgoing = outgoing.reshape(tile_count, SEND_MOST, row_width)
    sent_counts = jnp.sum(member, 0)[:, None]
    incoming, got_counts = (
        lax.all_to_all(outgoing, "tile", split_axis=0, concat_axis=0, tiled=True),
        lax.all_to_all(sent_counts, "tile", split_axis=0, concat_axis=0, tiled=True),
    )
    arrived = got_counts[:, 0]
    first_slot = jnp.cumsum(arrived) - arrived
    rank_list = jnp.arange(SEND_MOST)
    slot_ids = jnp.where(
        rank_list[None, :] < arrived[:, None], first_slot[:, None] + rank_list[None, :], MAXB
    ).reshape(-1)
    placer = (jnp.arange(MAXB)[:, None] == slot_ids[None, :]).astype(jnp.bfloat16)
    compact = jnp.dot(
        placer, incoming.reshape(-1, row_width), preferred_element_type=jnp.float32
    ).astype(jnp.bfloat16)
    matrices = beam_matrix[0, 0]
    slot_rows = compact.reshape(MAXB * BR, 2 * S)
    contract_dims = (((0,), (0,)), ((), ()))
    with_real = lax.dot_general(
        slot_rows, matrices[0], contract_dims, preferred_element_type=jnp.float32
    )
    with_imag = lax.dot_general(
        slot_rows, matrices[1], contract_dims, preferred_element_type=jnp.float32
    )
    image_re = with_real[:S] - with_imag[S:]
    image_im = with_real[S:] + with_imag[:S]
    partial_image = jnp.stack([image_re, image_im]).reshape(2, S, TZ, TX)
    summed = lax.psum_scatter(partial_image, "line", scatter_dimension=1, tiled=True)
    rimmed = with_halo(summed, (("tile", 2),), 2)
    return dip_apply(rimmed, dip_filter)


def solution(mesh):
    in_specs = (
        P("tile", "line", None),
        P("tile", None),
        P("line", "tile"),
        P("line", "tile", None, None, None),
        P(),
    )
    out_specs = P(None, "line", "tile", None)
    return jax.shard_map(
        per_device, mesh=mesh, in_specs=in_specs, out_specs=out_specs, check_vma=False
    )
```

profile of v0, /device:TPU:0, one launch (start us, length us, event | category | flops | bytes accessed | tf_op | source)
XLA Modules:
  0.0 124.6 jit_solution(10345511072185964696)
XLA Ops:
  6.5 0.7 slice_bitcast_fusion
  7.3 1.3 %collective-permute-start = (bf16[64,128]{1,0:T(8,128)(2,1)S(1)}, bf16[64,128]{1,0:T(8,128)(2,1)S(1)}, u32[]{:S(2)}, u32[]{:S(2)}) collective-permute-start(bf16[64,128]{1,0:T(8,128)(2,1)S(1)} %slice_bitcast_fusion), channel_id=1, source_target_pairs={{8,0},{16,8},{24,16},{9,1},{17,9},{25,17},{10,2},{18,10},{26,18},{... | collective-permute-start | bytes 49160 | tf_op jit(solution)/shard_map/ppermute | solution.py:19
  8.5 0.7 fusion.43
  9.3 0.8 fusion.44
  10.2 0.7 copy.13
  10.8 7.3 %all-to-all-start = ((s32[8,1,1]{2,1,0:T(1,128)}), s32[8,1,1]{2,1,0:T(1,128)S(1)}, u32[]{:S(2)}, u32[]{:S(2)}) async-start(s32[8,1,1]{2,1,0:T(1,128)} %copy.13), calls=%async_computation | async-start | bytes 8192 | tf_op jit(solution)/shard_map/all_to_all | solution.py:104
  19.3 0.7 cosine_bitcast_fusion
  20.6 0.7 fusion.45
  21.3 1.1 copy.14
  22.4 0.9 pad_maximum_fusion.3
  25.2 1.2 reshape.129
  26.4 6.0 %all-to-all-start.1 = ((bf16[8,4,16384]{2,1,0:T(4,128)(2,1)}), bf16[8,4,16384]{2,1,0:T(4,128)(2,1)S(1)}, u32[]{:S(2)}, u32[]{:S(2)}) async-start(bf16[8,4,16384]{2,1,0:T(4,128)(2,1)} %reshape.129), calls=%async_computation.1 | async-start | bytes 2097152 | tf_op jit(solution)/shard_map/all_to_all | solution.py:103
  33.1 25.9 %all-to-all-done.1 = bf16[8,4,16384]{2,1,0:T(4,128)(2,1)S(1)} async-done(((bf16[8,4,16384]{2,1,0:T(4,128)(2,1)}), bf16[8,4,16384]{2,1,0:T(4,128)(2,1)S(1)}, u32[]{:S(2)}, u32[]{:S(2)}) %all-to-all-start.1) | async-done | bytes 1048608 | tf_op jit(solution)/shard_map/all_to_all | solution.py:103
  60.2 4.7 %fusion = f32[128,1024]{1,0:T(8,128)S(1)} fusion(bf16[4096,128]{1,0:T(8,128)(2,1)S(1)} %reshape.131, bf16[1,1,2,4096,1024]{4,3,2,1,0:T(8,128)(2,1)} %param.8), kind=kOutput, calls=%fused_computation.2 | convolution fusion | flops 1073741824 | bytes 9961472 | tf_op jit(solution)/shard_map/dot_general | solution.py:122
  64.9 4.7 %fusion.2 = f32[128,1024]{1,0:T(8,128)S(1)} fusion(bf16[4096,128]{1,0:T(8,128)(2,1)S(1)} %reshape.131, bf16[1,1,2,4096,1024]{4,3,2,1,0:T(8,128)(2,1)} %param.8), kind=kOutput, calls=%fused_computation.4 | convolution fusion | flops 1073741824 | bytes 9961472 | tf_op jit(solution)/shard_map/dot_general | solution.py:119
  69.9 0.9 copy.26
  70.9 0.7 fusion.49
  71.6 20.1 %reduce-scatter.5.cloned.1.call-done = f32[16,2048]{1,0:T(8,128)} async-done(((f32[64,2048]{1,0:T(8,128)}), f32[16,2048]{1,0:T(8,128)}) %reduce-scatter.5.cloned.1.call-update) | async-done | bytes 131088
  91.7 0.9 copy.22
  92.7 1.3 %collective-permute-start.2 = (f32[2,16,2,128]{3,2,1,0:T(2,128)S(1)}, f32[2,16,2,128]{3,2,1,0:T(2,128)S(1)}, u32[]{:S(2)}, u32[]{:S(2)}) collective-permute-start(f32[2,16,2,128]{3,2,1,0:T(2,128)S(1)} %get-tuple-element.14), channel_id=1, source_target_pairs={{1,0},{2,1},{3,2},{4,3},{5,4},{6,5},{7,6},{9,8},{10,9},{11,10},{12... | collective-permute-start | bytes 98312 | tf_op jit(solution)/shard_map/ppermute | solution.py:32
  94.0 0.7 fusion.50
  94.7 4.5 %collective-permute-start.1 = (f32[2,16,2,128]{3,2,1,0:T(2,128)S(1)}, f32[2,16,2,128]{3,2,1,0:T(2,128)S(1)}, u32[]{:S(2)}, u32[]{:S(2)}) collective-permute-start(f32[2,16,2,128]{3,2,1,0:T(2,128)S(1)} %get-tuple-element.13), channel_id=1, source_target_pairs={{0,1},{1,2},{2,3},{3,4},{4,5},{5,6},{6,7},{8,9},{9,10},{10,11},{11... | collective-permute-start | bytes 98312 | tf_op jit(solution)/shard_map/ppermute | solution.py:30
  99.3 1.5 %collective-permute-done.1 = f32[2,16,2,128]{3,2,1,0:T(2,128)S(1)} collective-permute-done((f32[2,16,2,128]{3,2,1,0:T(2,128)S(1)}, f32[2,16,2,128]{3,2,1,0:T(2,128)S(1)}, u32[]{:S(2)}, u32[]{:S(2)}) %collective-permute-start.1) | collective-permute-done | bytes 32800 | tf_op jit(solution)/shard_map/ppermute | solution.py:30
  101.1 16.6 %fusion.35 = f32[2,16,8,128]{3,2,1,0:T(8,128)} fusion(f32[2,16,12,132]{3,2,1,0:T(8,128)S(1)} %select_maximum_fusion, f32[2,16,10,128]{3,2,1,0:T(8,128)S(1)} %constant_dynamic-update-slice_fusion, f32[2,16,8,128]{3,2,1,0:T(8,128)S(1)} %get-tuple-element.12, f32[2,16,2,128]{3,2,1,0:T(2,128)S(1)} %collective-permute-done.1, f32[]{:T(128)} %bitcast.39, ...), kind=kLoop, calls=%fused_computation.54 | loop fusion | flops 1671168 | bytes 3178596 | tf_op jit(solution)/shard_map/add | solution.py:69
  (37 shorter events, 5.6 us)
Async XLA Ops:
  7.3 15.1 %collective-permute-start = (bf16[64,128]{1,0:T(8,128)(2,1)S(1)}, bf16[64,128]{1,0:T(8,128)(2,1)S(1)}, u32[]{:S(2)}, u32[]{:S(2)}) collective-permute-start(bf16[64,128]{1,0:T(8,128)(2,1)S(1)} %slice_bitcast_fusion), channel_id=1, source_target_pairs={{8,0},{16,8},{24,16},{9,1},{17,9},{25,17},{10,2},{18,10},{26,18},{... | collective-permute-start | bytes 49160 | tf_op jit(solution)/shard_map/ppermute | solution.py:19
  10.8 15.6 %all-to-all-start = ((s32[8,1,1]{2,1,0:T(1,128)}), s32[8,1,1]{2,1,0:T(1,128)S(1)}, u32[]{:S(2)}, u32[]{:S(2)}) async-start(s32[8,1,1]{2,1,0:T(1,128)} %copy.13), calls=%async_computation | async-start | bytes 8192 | tf_op jit(solution)/shard_map/all_to_all | solution.py:104
  26.4 32.5 %all-to-all-start.1 = ((bf16[8,4,16384]{2,1,0:T(4,128)(2,1)}), bf16[8,4,16384]{2,1,0:T(4,128)(2,1)S(1)}, u32[]{:S(2)}, u32[]{:S(2)}) async-start(bf16[8,4,16384]{2,1,0:T(4,128)(2,1)} %reshape.129), calls=%async_computation.1 | async-start | bytes 2097152 | tf_op jit(solution)/shard_map/all_to_all | solution.py:103
  32.4 59.3 %reduce-scatter.5.cloned.1.call-start = ((), (), s32[]{:S(2)}) async-start(), calls=%async_computation.3 | async-start | bytes 655360
  64.9 6.0 %copy-start = (f32[5,5]{1,0:T(8,128)S(1)}, f32[5,5]{1,0:T(8,128)}, u32[]{:S(2)}) copy-start(f32[5,5]{1,0:T(8,128)} %param.9) | copy-start | bytes 304
  92.7 6.5 %collective-permute-start.2 = (f32[2,16,2,128]{3,2,1,0:T(2,128)S(1)}, f32[2,16,2,128]{3,2,1,0:T(2,128)S(1)}, u32[]{:S(2)}, u32[]{:S(2)}) collective-permute-start(f32[2,16,2,128]{3,2,1,0:T(2,128)S(1)} %get-tuple-element.14), channel_id=1, source_target_pairs={{1,0},{2,1},{3,2},{4,3},{5,4},{6,5},{7,6},{9,8},{10,9},{11,10},{12... | collective-permute-start | bytes 98312 | tf_op jit(solution)/shard_map/ppermute | solution.py:32
  94.7 6.1 %collective-permute-start.1 = (f32[2,16,2,128]{3,2,1,0:T(2,128)S(1)}, f32[2,16,2,128]{3,2,1,0:T(2,128)S(1)}, u32[]{:S(2)}, u32[]{:S(2)}) collective-permute-start(f32[2,16,2,128]{3,2,1,0:T(2,128)S(1)} %get-tuple-element.13), channel_id=1, source_target_pairs={{0,1},{1,2},{2,3},{3,4},{4,5},{5,6},{6,7},{8,9},{9,10},{10,11},{11... | collective-permute-start | bytes 98312 | tf_op jit(solution)/shard_map/ppermute | solution.py:30
Sparse Core Ops, SparseCore 0:
  71.0 20.6 reduce-scatter.4
where the time goes:
time: 126 us; the launch traced here: 125 us
  waiting for transfers between devices  47.6 us (38%)
  other arithmetic  22.9 us (18%)
  starting transfers between devices  20.4 us (16%)
  between operations  14.2 us (11%)
  matrix products  10.7 us (8%)
  local copies, waits for them, and re-layouts  8.75 us (7%)
    all_to_all x1, waiting for transfers between devices, per_device(): lax.all_to_all(outgoing, 'tile', split_axis=0, concat_axis=0, tiled=True)  25.9 us
    unnamed x2, waiting for transfers between devices  20.1 us
    add x1, other arithmetic, dip_apply(): result + dip_filter[down_step, side_step] * widened[:, :, down_step:down_...  16.6 us
    all_to_all x1, starting transfers between devices, per_device(): lax.all_to_all(sent_counts, 'tile', split_axis=0, concat_axis=0, tiled=True)  7.25 us
    all_to_all x1, starting transfers between devices, per_device(): lax.all_to_all(outgoing, 'tile', split_axis=0, concat_axis=0, tiled=True)  6 us
    dot_general x1, matrix products, per_device(): lax.dot_general(slot_rows, matrices[0], contract_dims, preferred_element_...  4.72 us
    dot_general x1, matrix products, per_device(): lax.dot_general(slot_rows, matrices[1], contract_dims, preferred_element_...  4.7 us
    ppermute x1, starting transfers between devices, with_halo(): lax.ppermute(tail, axis, [(i, (i + 1) % count) for i in range(ends)])  4.54 us
  transfers between devices with their start and end apart: 6, of which 3 were waited for; matrix products, arithmetic and copies ran while one was open for 10% of the time, Pallas kernels for 0%

commit v1 on v0

--- a/solution.py
+++ b/solution.py
@@ -90,7 +90,9 @@
     route_row = routes[0]
     peer_ids = jnp.arange(tile_count)
     member = (route_row[:, None] == peer_ids[None, :]).astype(jnp.int32)
-    before = jnp.cumsum(member, 0) - member
+    places = jnp.arange(member.shape[0])
+    earlier = (places[None, :] < places[:, None]).astype(jnp.int32)
+    before = jnp.sum(earlier[:, :, None] * member[None, :, :], 1)
     rank_in = jnp.sum(before * member, 1)
     send_slot = route_row * SEND_MOST + rank_in
     picker = (jnp.arange(tile_count * SEND_MOST)[:, None] == send_slot[None, :]).astype(
@@ -104,7 +106,7 @@
         lax.all_to_all(sent_counts, "tile", split_axis=0, concat_axis=0, tiled=True),
     )
     arrived = got_counts[:, 0]
-    first_slot = jnp.cumsum(arrived) - arrived
+    first_slot = jnp.sum(jnp.where(peer_ids[None, :] < peer_ids[:, None], arrived[None, :], 0), 1)
     rank_list = jnp.arange(SEND_MOST)
     slot_ids = jnp.where(
         rank_list[None, :] < arrived[:, None], first_slot[:, None] + rank_list[None, :], MAXB

time: 126 us -> 127 us (level)
  no operation moved by 1% of the time
where the time goes in v1:
time: 127 us; the launch traced here: 125 us
  waiting for transfers between devices  47.7 us (38%)
  other arithmetic  23.1 us (18%)
  starting transfers between devices  20.4 us (16%)
  between operations  14.3 us (11%)
  matrix products  10.8 us (9%)
  local copies, waits for them, and re-layouts  8.82 us (7%)
    all_to_all x1, waiting for transfers between devices, per_device(): lax.all_to_all(outgoing, 'tile', split_axis=0, concat_axis=0, tiled=True)  25.9 us
    unnamed x2, waiting for transfers between devices  20.2 us
    add x1, other arithmetic, dip_apply(): result + dip_filter[down_step, side_step] * widened[:, :, down_step:down_...  16.6 us
    all_to_all x1, starting transfers between devices, per_device(): lax.all_to_all(sent_counts, 'tile', split_axis=0, concat_axis=0, tiled=True)  7.25 us
    all_to_all x1, starting transfers between devices, per_device(): lax.all_to_all(outgoing, 'tile', split_axis=0, concat_axis=0, tiled=True)  5.98 us
    dot_general x1, matrix products, per_device(): lax.dot_general(slot_rows, matrices[0], contract_dims, preferred_element_...  4.72 us
    dot_general x1, matrix products, per_device(): lax.dot_general(slot_rows, matrices[1], contract_dims, preferred_element_...  4.7 us
    ppermute x1, starting transfers between devices, with_halo(): lax.ppermute(tail, axis, [(i, (i + 1) % count) for i in range(ends)])  4.54 us
  transfers between devices with their start and end apart: 6, of which 3 were waited for; matrix products, arithmetic and copies ran while one was open for 10% of the time, Pallas kernels for 0%

profile of v1, /device:TPU:0, one launch (start us, length us, event | category | flops | bytes accessed | tf_op | source)
XLA Modules:
  0.0 125.0 jit_solution(16368564808872789891)
XLA Ops:
  6.5 0.7 slice_bitcast_fusion
  7.3 1.3 %collective-permute-start = (bf16[64,128]{1,0:T(8,128)(2,1)S(1)}, bf16[64,128]{1,0:T(8,128)(2,1)S(1)}, u32[]{:S(2)}, u32[]{:S(2)}) collective-permute-start(bf16[64,128]{1,0:T(8,128)(2,1)S(1)} %slice_bitcast_fusion), channel_id=1, source_target_pairs={{8,0},{16,8},{24,16},{9,1},{17,9},{25,17},{10,2},{18,10},{26,18},{... | collective-permute-start | bytes 49160 | tf_op jit(solution)/shard_map/ppermute | solution.py:19
  8.6 0.7 fusion.43
  9.7 0.9 fusion.45
  10.6 0.7 copy.18
  11.2 7.3 %all-to-all-start = ((s32[8,1,1]{2,1,0:T(1,128)}), s32[8,1,1]{2,1,0:T(1,128)S(1)}, u32[]{:S(2)}, u32[]{:S(2)}) async-start(s32[8,1,1]{2,1,0:T(1,128)} %copy.18), calls=%async_computation | async-start | bytes 8192 | tf_op jit(solution)/shard_map/all_to_all | solution.py:106
  19.8 0.7 cosine_bitcast_fusion
  21.0 0.7 fusion.46
  21.7 1.1 copy.21
  22.8 0.9 pad_maximum_fusion.3
  25.6 1.2 reshape.135
  26.9 6.0 %all-to-all-start.1 = ((bf16[8,4,16384]{2,1,0:T(4,128)(2,1)}), bf16[8,4,16384]{2,1,0:T(4,128)(2,1)S(1)}, u32[]{:S(2)}, u32[]{:S(2)}) async-start(bf16[8,4,16384]{2,1,0:T(4,128)(2,1)} %reshape.135), calls=%async_computation.1 | async-start | bytes 2097152 | tf_op jit(solution)/shard_map/all_to_all | solution.py:105
  33.4 25.9 %all-to-all-done.1 = bf16[8,4,16384]{2,1,0:T(4,128)(2,1)S(1)} async-done(((bf16[8,4,16384]{2,1,0:T(4,128)(2,1)}), bf16[8,4,16384]{2,1,0:T(4,128)(2,1)S(1)}, u32[]{:S(2)}, u32[]{:S(2)}) %all-to-all-start.1) | async-done | bytes 1048608 | tf_op jit(solution)/shard_map/all_to_all | solution.py:105
  60.6 4.7 %fusion = f32[128,1024]{1,0:T(8,128)S(1)} fusion(bf16[4096,128]{1,0:T(8,128)(2,1)S(1)} %reshape.137, bf16[1,1,2,4096,1024]{4,3,2,1,0:T(8,128)(2,1)} %param.8), kind=kOutput, calls=%fused_computation.2 | convolution fusion | flops 1073741824 | bytes 9961472 | tf_op jit(solution)/shard_map/dot_general | solution.py:124
  65.3 4.7 %fusion.2 = f32[128,1024]{1,0:T(8,128)S(1)} fusion(bf16[4096,128]{1,0:T(8,128)(2,1)S(1)} %reshape.137, bf16[1,1,2,4096,1024]{4,3,2,1,0:T(8,128)(2,1)} %param.8), kind=kOutput, calls=%fused_computation.4 | convolution fusion | flops 1073741824 | bytes 9961472 | tf_op jit(solution)/shard_map/dot_general | solution.py:121
  70.3 0.9 copy.35
  71.3 0.7 fusion.50
  72.0 20.2 %reduce-scatter.5.cloned.1.call-done = f32[16,2048]{1,0:T(8,128)} async-done(((f32[64,2048]{1,0:T(8,128)}), f32[16,2048]{1,0:T(8,128)}) %reduce-scatter.5.cloned.1.call-update) | async-done | bytes 131088
  92.2 0.9 copy.31
  93.1 1.3 %collective-permute-start.2 = (f32[2,16,2,128]{3,2,1,0:T(2,128)S(1)}, f32[2,16,2,128]{3,2,1,0:T(2,128)S(1)}, u32[]{:S(2)}, u32[]{:S(2)}) collective-permute-start(f32[2,16,2,128]{3,2,1,0:T(2,128)S(1)} %get-tuple-element.14), channel_id=1, source_target_pairs={{1,0},{2,1},{3,2},{4,3},{5,4},{6,5},{7,6},{9,8},{10,9},{11,10},{12... | collective-permute-start | bytes 98312 | tf_op jit(solution)/shard_map/ppermute | solution.py:32
  94.4 0.7 fusion.51
  95.1 4.5 %collective-permute-start.1 = (f32[2,16,2,128]{3,2,1,0:T(2,128)S(1)}, f32[2,16,2,128]{3,2,1,0:T(2,128)S(1)}, u32[]{:S(2)}, u32[]{:S(2)}) collective-permute-start(f32[2,16,2,128]{3,2,1,0:T(2,128)S(1)} %get-tuple-element.13), channel_id=1, source_target_pairs={{0,1},{1,2},{2,3},{3,4},{4,5},{5,6},{6,7},{8,9},{9,10},{10,11},{11... | collective-permute-start | bytes 98312 | tf_op jit(solution)/shard_map/ppermute | solution.py:30
  99.7 1.5 %collective-permute-done.1 = f32[2,16,2,128]{3,2,1,0:T(2,128)S(1)} collective-permute-done((f32[2,16,2,128]{3,2,1,0:T(2,128)S(1)}, f32[2,16,2,128]{3,2,1,0:T(2,128)S(1)}, u32[]{:S(2)}, u32[]{:S(2)}) %collective-permute-start.1) | collective-permute-done | bytes 32800 | tf_op jit(solution)/shard_map/ppermute | solution.py:30
  101.6 16.6 %fusion.35 = f32[2,16,8,128]{3,2,1,0:T(8,128)} fusion(f32[2,16,12,132]{3,2,1,0:T(8,128)S(1)} %select_maximum_fusion, f32[2,16,10,128]{3,2,1,0:T(8,128)S(1)} %constant_dynamic-update-slice_fusion, f32[2,16,8,128]{3,2,1,0:T(8,128)S(1)} %get-tuple-element.12, f32[2,16,2,128]{3,2,1,0:T(2,128)S(1)} %collective-permute-done.1, f32[]{:T(128)} %bitcast.38, ...), kind=kLoop, calls=%fused_computation.54 | loop fusion | flops 1671168 | bytes 3178596 | tf_op jit(solution)/shard_map/add | solution.py:69
  (38 shorter events, 5.9 us)
Async XLA Ops:
  7.3 15.5 %collective-permute-start = (bf16[64,128]{1,0:T(8,128)(2,1)S(1)}, bf16[64,128]{1,0:T(8,128)(2,1)S(1)}, u32[]{:S(2)}, u32[]{:S(2)}) collective-permute-start(bf16[64,128]{1,0:T(8,128)(2,1)S(1)} %slice_bitcast_fusion), channel_id=1, source_target_pairs={{8,0},{16,8},{24,16},{9,1},{17,9},{25,17},{10,2},{18,10},{26,18},{... | collective-permute-start | bytes 49160 | tf_op jit(solution)/shard_map/ppermute | solution.py:19
  11.2 15.6 %all-to-all-start = ((s32[8,1,1]{2,1,0:T(1,128)}), s32[8,1,1]{2,1,0:T(1,128)S(1)}, u32[]{:S(2)}, u32[]{:S(2)}) async-start(s32[8,1,1]{2,1,0:T(1,128)} %copy.18), calls=%async_computation | async-start | bytes 8192 | tf_op jit(solution)/shard_map/all_to_all | solution.py:106
  26.9 32.5 %all-to-all-start.1 = ((bf16[8,4,16384]{2,1,0:T(4,128)(2,1)}), bf16[8,4,16384]{2,1,0:T(4,128)(2,1)S(1)}, u32[]{:S(2)}, u32[]{:S(2)}) async-start(bf16[8,4,16384]{2,1,0:T(4,128)(2,1)} %reshape.135), calls=%async_computation.1 | async-start | bytes 2097152 | tf_op jit(solution)/shard_map/all_to_all | solution.py:105
  32.8 59.3 %reduce-scatter.5.cloned.1.call-start = ((), (), s32[]{:S(2)}) async-start(), calls=%async_computation.3 | async-start | bytes 655360
  65.3 6.0 %copy-start = (f32[5,5]{1,0:T(8,128)S(1)}, f32[5,5]{1,0:T(8,128)}, u32[]{:S(2)}) copy-start(f32[5,5]{1,0:T(8,128)} %param.9) | copy-start | bytes 304
  93.1 6.5 %collective-permute-start.2 = (f32[2,16,2,128]{3,2,1,0:T(2,128)S(1)}, f32[2,16,2,128]{3,2,1,0:T(2,128)S(1)}, u32[]{:S(2)}, u32[]{:S(2)}) collective-permute-start(f32[2,16,2,128]{3,2,1,0:T(2,128)S(1)} %get-tuple-element.14), channel_id=1, source_target_pairs={{1,0},{2,1},{3,2},{4,3},{5,4},{6,5},{7,6},{9,8},{10,9},{11,10},{12... | collective-permute-start | bytes 98312 | tf_op jit(solution)/shard_map/ppermute | solution.py:32
  95.1 6.1 %collective-permute-start.1 = (f32[2,16,2,128]{3,2,1,0:T(2,128)S(1)}, f32[2,16,2,128]{3,2,1,0:T(2,128)S(1)}, u32[]{:S(2)}, u32[]{:S(2)}) collective-permute-start(f32[2,16,2,128]{3,2,1,0:T(2,128)S(1)} %get-tuple-element.13), channel_id=1, source_target_pairs={{0,1},{1,2},{2,3},{3,4},{4,5},{5,6},{6,7},{8,9},{9,10},{10,11},{11... | collective-permute-start | bytes 98312 | tf_op jit(solution)/shard_map/ppermute | solution.py:30
Sparse Core Ops, SparseCore 0:
  71.4 20.7 reduce-scatter.4

commit v2 on v0

v2 whole, which is shorter than its diff:
```python
import functools

import jax
import jax.numpy as jnp
import numpy as np
from jax import lax
from jax.experimental import pallas as pl
from jax.experimental.pallas import tpu as pltpu
from jax.sharding import PartitionSpec as P

P_SIZE = 256
WIN = 128
BR = 128
LANES = 128
CW = 256
MESH = pl.DeviceIdType.MESH


def slant_tables(freq_count):
    f32 = np.float32
    slopes = np.arange(P_SIZE, dtype=f32) - f32(P_SIZE / 2)
    offsets = np.arange(WIN, dtype=f32) - f32((WIN - 1) / 2)
    taper = np.exp(f32(-0.5) * (offsets / f32(0.4 * WIN)) ** 2)
    taper = taper / np.sqrt(np.sum(taper * taper))
    out = np.zeros((freq_count, 2, P_SIZE // BR, 2 * WIN, BR), f32)
    for f in range(freq_count):
        factor = f32(2.0) + f32(f) / f32(freq_count)
        angle = f32(np.pi) * factor * slopes[:, None] * offsets[None, :] / f32(WIN)
        re, im = taper * np.cos(angle), -taper * np.sin(angle)
        for odd in range(2):
            shift = odd * (WIN // 2)
            both = np.concatenate([np.roll(re, shift, 1), np.roll(im, shift, 1)], 1)
            for q in range(P_SIZE // BR):
                out[f, odd, q] = both[q * BR : (q + 1) * BR].T
    return out.reshape(-1, 2 * WIN, BR)


def kernel(
    n_line, n_tile, n_block, n_slot, n_shot,
    traces, codes, routes, dip, table_hbm, beam_hbm, out,
    tiles, halo, meta, table, beam, slots_v, slots, cosine, sine, stacked, part, r_main, r_top, r_bot,
    local, main_send, main_recv, halo_send, halo_recv, head_send, head_recv, meta_send, meta_recv,
    part_send, part_recv, top_send, top_recv, bot_send, bot_recv,
):
    line, tile = lax.axis_index("line"), lax.axis_index("tile")
    n_z = n_tile // 2
    z, x = tile // 2, tile % 2
    half = WIN // 2
    n_full = traces.shape[0] // LANES
    shots = n_shot // n_line
    depth = n_slot * BR
    pieces = out.shape[1] * LANES // CW

    fetches = [pltpu.make_async_copy(table_hbm, table, local.at[0])]
    for i in range(4):
        rows = pl.ds(i * (2 * depth // 4), 2 * depth // 4)
        fetches.append(pltpu.make_async_copy(beam_hbm.at[rows], beam.at[rows], local.at[1 + i]))
    for fetch in fetches:
        fetch.start()

    barrier = pltpu.get_barrier_semaphore()

    def greet(to_line, to_tile):
        pl.semaphore_signal(barrier, inc=1, device_id=(to_line, to_tile), device_id_type=MESH)

    for k in range(1, n_tile):
        greet(line, lax.rem(tile + k, n_tile))
    for k in range(1, n_line):
        other = lax.rem(line + k, n_line)
        greet(other, tile)

        @pl.when(tile > 0)
        def _():
            greet(other, tile - 1)

        @pl.when(tile < n_tile - 1)
        def _():
            greet(other, tile + 1)

    for i in range(n_full):
        tiles[tile, i] = jnp.transpose(traces[i * LANES : (i + 1) * LANES, :])
    meta[tile] = jnp.zeros((8, LANES), jnp.int32)
    meta[tile, 0:1, 0:n_block] = routes[...]
    meta[tile, 1:2, 0:n_shot] = codes[...]
    meta[tile, 1:2, n_shot : 2 * n_shot] = codes[...]

    @pl.when(line == n_line - 1)
    def _():
        halo[tile] = jnp.zeros((half, LANES), jnp.bfloat16)

    @pl.when(tile == 0)
    def _():
        r_top[...] = jnp.zeros_like(r_top)

    @pl.when(tile == n_tile - 1)
    def _():
        r_bot[...] = jnp.zeros_like(r_bot)

    greeted = n_tile - 1 + (n_line - 1) * (
        1 + (tile > 0).astype(jnp.int32) + (tile < n_tile - 1).astype(jnp.int32)
    )
    pl.semaphore_wait(barrier, greeted)

    def remote(src, dst, send, recv, to_line, to_tile):
        return pltpu.make_async_remote_copy(
            src_ref=src, dst_ref=dst, send_sem=send, recv_sem=recv,
            device_id=(to_line, to_tile), device_id_type=MESH,
        )

    def main_copy(source, way, to_tile):
        block = tiles.at[source, pl.ds(0, n_full)]
        return remote(block, block, main_send.at[source, way], main_recv.at[source], line, to_tile)

    def halo_copy(source, way, to_tile):
        block = halo.at[source]
        return remote(block, block, halo_send.at[source, way], halo_recv.at[source], line, to_tile)

    across = z * 2 + 1 - x
    head_out = remote(
        traces.at[pl.ds(0, half)], halo.at[tile], head_send, head_recv, jnp.maximum(line - 1, 0), tile
    )
    meta_out = [
        remote(meta.at[tile], meta.at[tile], meta_send.at[k], meta_recv.at[tile], line, lax.rem(tile + k, n_tile))
        for k in range(1, n_tile)
    ]

    def onward(copy, step, way, act):
        come_from = z - step * way
        source = come_from * 2 + x

        @pl.when((come_from >= 0) & (come_from < n_z))
        def _():
            if act == "start" and step:
                copy(source, 0, across).wait_recv()
            for slot, to in ((0, 1), (1, -1)):
                if step and to != way:
                    continue

                @pl.when((z + to >= 0) & (z + to < n_z))
                def _():
                    c = copy(source, slot, (z + to) * 2 + x)
                    c.start() if act == "start" else c.wait_send()

            c = copy(source, 2, across)
            c.start() if act == "start" else c.wait_send()

    @pl.when(line > 0)
    def _():
        head_out.start()

    for c in meta_out:
        c.start()
    onward(main_copy, 0, 1, "start")

    @pl.when(line < n_line - 1)
    def _():
        head_out.wait_recv()

    onward(halo_copy, 0, 1, "start")

    for k in range(1, n_tile):
        source = lax.rem(tile + k, n_tile)
        remote(meta.at[source], meta.at[source], meta_send.at[k], meta_recv.at[source], line, source).wait_recv()
    lane_row = lax.broadcasted_iota(jnp.int32, (8, LANES), 1)
    wanted = lax.broadcasted_iota(jnp.int32, (n_slot, LANES), 0)
    lane_slots = lax.broadcasted_iota(jnp.int32, (n_slot, LANES), 1)
    found = jnp.zeros((n_slot, LANES), jnp.int32)
    before = jnp.zeros((1, 1), jnp.int32)
    for f in range(n_tile):
        row = meta[f]
        member = jnp.where((lane_row < n_block) & (row == tile), 1, 0)
        upto = member
        step = 1
        while step < n_block:
            upto = upto + jnp.where(lane_row >= step, pltpu.roll(upto, step, 1), 0)
            step *= 2
        rank = jnp.where(member > 0, upto - member + before, -1)
        found = found + jnp.where(
            jnp.broadcast_to(rank[0:1], (n_slot, LANES)) == wanted, lane_slots + (f * n_block + 1), 0
        )
        before = before + jnp.sum(member[0:1], axis=1, keepdims=True)
        angle = 2.0 * jnp.pi * row[1:2].astype(jnp.float32) / 256.0
        upright = jnp.transpose(jnp.broadcast_to(angle, (LANES, LANES)))
        sign = jnp.where(lax.broadcasted_iota(jnp.int32, (LANES, LANES), 0) < n_shot, 1.0, -1.0)
        cosine[f] = upright
        sine[f] = sign
    slots_v[...] = jnp.broadcast_to(jnp.sum(found, axis=1, keepdims=True), (n_slot, LANES))
    to_scalars = pltpu.make_async_copy(slots_v, slots, local.at[5])
    to_scalars.start()

    for step in range(1, n_z):
        for way in (1, -1):
            onward(main_copy, step, way, "start")
        for way in (1, -1):
            onward(halo_copy, step, way, "start")

    def phases(f, carry):
        angle = cosine[f]
        sine[f] = sine[f] * jnp.sin(angle)
        cosine[f] = jnp.cos(angle)
        return carry

    lax.fori_loop(0, n_tile, phases, 0)

    for place in range(n_z):
        source = place * 2 + 1 - x
        main_copy(source, 0, across).wait_recv()
        halo_copy(source, 0, across).wait_recv()
    for f in range(n_tile):
        rim = jnp.concatenate([halo[f], jnp.zeros((LANES - half, LANES), jnp.bfloat16)], 0)
        tiles[f, n_full] = jnp.transpose(rim)
    to_scalars.wait()
    fetches[0].wait()

    first_half = lax.broadcasted_iota(jnp.int32, (LANES, LANES), 1) < half

    def swapped(value):
        return jnp.concatenate([value[n_shot:], value[:n_shot]], 0)

    def turned(value):
        return jnp.concatenate([-value[n_shot:], value[:n_shot]], 0)

    def one_slot(n, carry):
        name = slots[n, 0]
        there = jnp.where(name > 0, 1.0, 0.0)
        block = jnp.maximum(name - 1, 0)
        f = block // n_block
        b = block - f * n_block
        window = b // 2
        data = jnp.where(first_half, tiles[f, (window + 1) // 2], tiles[f, window // 2])
        lhs = jnp.concatenate([data, turned(data)], 1)
        raw = jnp.dot(lhs, table[f * 4 + b % 4], preferred_element_type=jnp.float32)
        beam_now = ((raw * cosine[f] + swapped(raw) * sine[f]) * there)
        at = pl.multiple_of(n * BR, BR)
        stacked[:, pl.ds(at, BR)] = beam_now.astype(jnp.bfloat16)
        stacked[:, pl.ds(pl.multiple_of(at + depth, BR), BR)] = turned(beam_now).astype(jnp.bfloat16)
        return carry

    lax.fori_loop(0, n_slot, one_slot, 0)

    for fetch in fetches[1:]:
        fetch.wait()

    def piece_copy(k, j):
        to = lax.rem(line + k, n_line)
        cols = pl.ds(j * CW, CW)
        return remote(
            part.at[to, :, cols], r_main.at[k - 1, :, cols], part_send.at[k - 1, j], part_recv.at[k - 1, j], to, tile
        )

    def edge_copy(k, up):
        to = lax.rem(line + k, n_line)
        if up:
            return remote(
                part.at[to, :, pl.ds(0, CW)], r_bot.at[k], top_send.at[k], bot_recv.at[k], to,
                jnp.maximum(tile - 1, 0),
            )
        return remote(
            part.at[to, :, pl.ds((pieces - 1) * CW, CW)], r_top.at[k], bot_send.at[k], top_recv.at[k], to,
            jnp.minimum(tile + 1, n_tile - 1),
        )

    for j in [0, pieces - 1, *range(1, pieces - 1)]:
        image = jnp.dot(stacked[...], beam[:, j * CW : (j + 1) * CW], preferred_element_type=jnp.float32)
        for to in range(n_line):
            low = to * shots
            part[to, :, j * CW : (j + 1) * CW] = jnp.concatenate(
                [image[low : low + shots], image[n_shot + low : n_shot + low + shots]], 0
            ).astype(jnp.bfloat16)
        if j == 0:

            @pl.when(tile > 0)
            def _():
                for k in range(n_line):
                    edge_copy(k, True).start()

        if j == pieces - 1:

            @pl.when(tile < n_tile - 1)
            def _():
                for k in range(n_line):
                    edge_copy(k, False).start()

        for k in range(1, n_line):
            piece_copy(k, j).start()

    @pl.when(line > 0)
    def _():
        head_out.wait_send()

    for c in meta_out:
        c.wait_send()
    for copy in (main_copy, halo_copy):
        onward(copy, 0, 1, "wait")
        for step in range(1, n_z):
            for way in (1, -1):
                onward(copy, step, way, "wait")

    @pl.when(tile > 0)
    def _():
        for k in range(n_line):
            edge_copy(k, False).wait_recv()
            edge_copy(k, True).wait_send()

    @pl.when(tile < n_tile - 1)
    def _():
        for k in range(n_line):
            edge_copy(k, True).wait_recv()
            edge_copy(k, False).wait_send()

    for j in range(pieces):
        for k in range(1, n_line):
            piece_copy(k, j).wait()

    wide = jnp.float32
    image_rows = []
    top = sum(r_top[k].astype(wide) for k in range(n_line))
    bottom = sum(r_bot[k].astype(wide) for k in range(n_line))
    image_rows += [top[:, :LANES], top[:, LANES:]]
    for row in range(out.shape[1]):
        cols = slice(row * LANES, (row + 1) * LANES)
        total = part[line, :, cols].astype(wide)
        for k in range(n_line - 1):
            total = total + r_main[k, :, cols].astype(wide)
        image_rows.append(total)
    image_rows += [bottom[:, :LANES], bottom[:, LANES:]]
    lane = lax.broadcasted_iota(jnp.int32, image_rows[0].shape, 1)
    for row in range(out.shape[1]):
        result = None
        for side in range(5):
            column = sum(dip[down, side] * image_rows[row + down] for down in range(5))
            move = side - 2
            if move:
                column = pltpu.roll(column, (-move) % LANES, 1)
                column = jnp.where((lane + move >= 0) & (lane + move < LANES), column, 0.0)
            result = column if result is None else result + column
        out[:, row, :] = result


def per_device(traces, codes, routes, beam_matrix, dip_filter):
    n_line, n_tile = lax.axis_size("line"), lax.axis_size("tile")
    n_shot = codes.shape[1]
    n_block = routes.shape[1]
    depth, pixels = beam_matrix.shape[3:]
    n_slot = depth // BR
    n_full = traces.shape[1] // LANES
    rows = 2 * (n_shot // n_line)
    tall = pixels // LANES
    pieces = pixels // CW
    table = jnp.asarray(slant_tables(n_tile)).astype(jnp.bfloat16)
    bf16, f32, i32 = jnp.bfloat16, jnp.float32, jnp.int32
    dma = pltpu.SemaphoreType.DMA
    vmem = pl.BlockSpec(memory_space=pltpu.VMEM)
    hbm = pl.BlockSpec(memory_space=pl.ANY)
    result = pl.pallas_call(
        functools.partial(kernel, n_line, n_tile, n_block, n_slot, n_shot),
        out_shape=jax.ShapeDtypeStruct((rows, tall, LANES), f32),
        in_specs=[vmem, vmem, vmem, pl.BlockSpec(memory_space=pltpu.SMEM), hbm, hbm],
        out_specs=vmem,
        scratch_shapes=[
            pltpu.VMEM((n_tile, n_full + 1, LANES, LANES), bf16),
            pltpu.VMEM((n_tile, WIN // 2, LANES), bf16),
            pltpu.VMEM((n_tile, 8, LANES), i32),
            pltpu.VMEM(table.shape, bf16),
            pltpu.VMEM((2 * depth, pixels), bf16),
            pltpu.VMEM((n_slot, LANES), i32),
            pltpu.SMEM((n_slot, LANES), i32),
            pltpu.VMEM((n_tile, LANES, LANES), f32),
            pltpu.VMEM((n_tile, LANES, LANES), f32),
            pltpu.VMEM((2 * n_shot, 2 * depth), bf16),
            pltpu.VMEM((n_line, rows, pixels), bf16),
            pltpu.VMEM((n_line - 1, rows, pixels), bf16),
            pltpu.VMEM((n_line, rows, CW), bf16),
            pltpu.VMEM((n_line, rows, CW), bf16),
            dma((6,)),
            dma((n_tile, 3)), dma((n_tile,)),
            dma((n_tile, 3)), dma((n_tile,)),
            dma, dma,
            dma((n_tile,)), dma((n_tile,)),
            dma((n_line - 1, pieces)), dma((n_line - 1, pieces)),
            dma((n_line,)), dma((n_line,)),
            dma((n_line,)), dma((n_line,)),
        ],
        compiler_params=pltpu.CompilerParams(
            collective_id=0, has_side_effects=True, vmem_limit_bytes=50 * 2**20
        ),
    )(traces[0], codes, routes, dip_filter, table, beam_matrix.reshape(2 * depth, pixels))
    return result.reshape(2, rows // 2, tall, LANES)


def solution(mesh):
    in_specs = (
        P("tile", "line", None),
        P("tile", None),
        P("line", "tile"),
        P("line", "tile", None, None, None),
        P(),
    )
    out_specs = P(None, "line", "tile", None)
    return jax.shard_map(
        per_device, mesh=mesh, in_specs=in_specs, out_specs=out_specs, check_vma=False
    )
```

time: 126 us -> 44.7 us (0.35)
  waiting for transfers between devices: 47.6 us -> 0 us
  Pallas kernels: 0 us -> 39.3 us
  other arithmetic: 22.9 us -> 0 us
  starting transfers between devices: 20.4 us -> 0 us
  between operations: 14.2 us -> 0.01 us
  matrix products: 10.7 us -> 0 us
  local copies, waits for them, and re-layouts: 8.75 us -> 5.15 us
    pallas_call x0 -> x1, Pallas kernels: none -> 39.3 us  [per_device(): pl.pallas_call(functools.partial(kernel, n_line, n_tile, n_block, n_slot,...]
    all_to_all x2 -> x0, waiting for transfers between devices: 25.9 us -> none  [the longest x1 25.9 us: per_device(): lax.all_to_all(outgoing, 'tile', split_axis=0, concat_axis=0, tiled=True)]
    unnamed x2 -> x0, waiting for transfers between devices: 20.1 us -> none
    add x1 -> x0, other arithmetic: 16.6 us -> none  [dip_apply(): result + dip_filter[down_step, side_step] * widened[:, :, down_step:down_...]
    all_to_all x2 -> x0, starting transfers between devices: 13.3 us -> none  [the longest x1 7.25 us: per_device(): lax.all_to_all(sent_counts, 'tile', split_axis=0, concat_axis=0, tiled=True)]
    dot_general x5 -> x0, matrix products: 10.7 us -> none  [the longest x1 4.72 us: per_device(): lax.dot_general(slot_rows, matrices[0], contract_dims, preferred_element_...]
    ppermute x3 -> x0, starting transfers between devices: 7.11 us -> none  [the longest x1 4.54 us: with_halo(): lax.ppermute(tail, axis, [(i, (i + 1) % count) for i in range(ends)])]
    slice x6 -> x0, local copies, waits for them, and re-layouts: 3.41 us -> none  [the longest x2 1.38 us: dip_apply(): dip_filter[down_step, side_step]]
  transfers between devices with their start and end apart: 6 -> 0, of which waited for: 3 -> 0; matrix products, arithmetic and copies ran while one was open for 10% -> 0% of each run, Pallas kernels for 0% -> 0%
where the time goes in v2:
time: 44.7 us; the launch traced here: 44.5 us
  Pallas kernels  39.3 us (88%)
  local copies, waits for them, and re-layouts  5.15 us (12%)
    pallas_call x1, Pallas kernels, per_device(): pl.pallas_call(functools.partial(kernel, n_line, n_tile, n_block, n_slot,...  39.3 us
    unnamed x11, local copies, waits for them, and re-layouts  5.15 us

profile of v2, /device:TPU:0, one launch (start us, length us, event | category | flops | bytes accessed | tf_op | source)
XLA Modules:
  0.0 44.5 jit_solution(9680144489174112263)
XLA Ops:
  0.0 0.0 copy-start
  0.0 1.6 %copy-done = bf16[32,256,128]{2,1,0:T(8,128)(2,1)S(1)} copy-done((bf16[32,256,128]{2,1,0:T(8,128)(2,1)S(1)}, bf16[32,256,128]{2,1,0:T(8,128)(2,1)}, u32[]{:S(2)}) %copy-start) | copy-done | bytes 2097176
  1.6 0.0 copy-start.1
  1.6 0.9 %copy-done.1 = bf16[1,512,128]{2,1,0:T(8,128)(2,1)S(1)} copy-done((bf16[1,512,128]{2,1,0:T(8,128)(2,1)S(1)}, bf16[1,512,128]{2,1,0:T(8,128)(2,1)}, u32[]{:S(2)}) %copy-start.1) | copy-done | bytes 131096
  2.5 0.0 copy-start.2
  2.5 0.7 %copy-done.2 = f32[5,5]{1,0:T(8,128)S(1)} copy-done((f32[5,5]{1,0:T(8,128)S(1)}, f32[5,5]{1,0:T(8,128)}, u32[]{:S(2)}) %copy-start.2) | copy-done | bytes 124
  3.2 0.0 copy-start.3
  3.2 0.7 %copy-done.3 = s32[1,64]{1,0:T(1,128)S(1)} copy-done((s32[1,64]{1,0:T(1,128)S(1)}, s32[1,64]{1,0:T(1,128)}, u32[]{:S(2)}) %copy-start.3) | copy-done | bytes 280
  3.8 0.0 copy-start.4
  3.8 0.7 %copy-done.4 = s32[1,16]{1,0:T(1,128)S(1)} copy-done((s32[1,16]{1,0:T(1,128)S(1)}, s32[1,16]{1,0:T(1,128)}, u32[]{:S(2)}) %copy-start.4) | copy-done | bytes 88
  4.5 39.3 %shard_map.64 = f32[32,8,128]{2,1,0:T(8,128)S(1)} custom-call(bf16[512,128]{1,0:T(8,128)(2,1)S(1)} %bitcast.4, s32[1,64]{1,0:T(1,128)S(1)} %copy-done.3, s32[1,16]{1,0:T(1,128)S(1)} %copy-done.4, f32[5,5]{1,0:T(8,128)S(1)} %copy-done.2, bf16[32,256,128]{2,1,0:T(8,128)(2,1)S(1)} %copy-done, bf16[8192,1024]{1,0:T(8,128)(2,1)} %bitcast.5), custom_call_target="tpu_custom_call" | custom-call | tf_op jit(solution)/shard_map/pallas_call | solution.py:355
  43.8 0.7 %copy.8 = f32[2,16,8,128]{3,2,1,0:T(8,128)} copy(f32[2,16,8,128]{3,2,1,0:T(8,128)S(1)} %bitcast.3) | data formatting | bytes 262144
Async XLA Ops:
  0.0 1.6 %copy-start = (bf16[32,256,128]{2,1,0:T(8,128)(2,1)S(1)}, bf16[32,256,128]{2,1,0:T(8,128)(2,1)}, u32[]{:S(2)}) copy-start(bf16[32,256,128]{2,1,0:T(8,128)(2,1)} %constant.7.table_hbm) | copy-start | bytes 6291460
  1.6 0.9 %copy-start.1 = (bf16[1,512,128]{2,1,0:T(8,128)(2,1)S(1)}, bf16[1,512,128]{2,1,0:T(8,128)(2,1)}, u32[]{:S(2)}) copy-start(bf16[1,512,128]{2,1,0:T(8,128)(2,1)} %param.6) | copy-start | bytes 393220
  2.5 0.7 %copy-start.2 = (f32[5,5]{1,0:T(8,128)S(1)}, f32[5,5]{1,0:T(8,128)}, u32[]{:S(2)}) copy-start(f32[5,5]{1,0:T(8,128)} %dip.1) | copy-start | bytes 304
  3.2 0.7 %copy-start.3 = (s32[1,64]{1,0:T(1,128)S(1)}, s32[1,64]{1,0:T(1,128)}, u32[]{:S(2)}) copy-start(s32[1,64]{1,0:T(1,128)} %codes.1) | copy-start | bytes 772
  3.8 0.7 %copy-start.4 = (s32[1,16]{1,0:T(1,128)S(1)}, s32[1,16]{1,0:T(1,128)}, u32[]{:S(2)}) copy-start(s32[1,16]{1,0:T(1,128)} %routes.1) | copy-start | bytes 196

commit v3 on v2

--- a/solution.py
+++ b/solution.py
@@ -37,8 +37,8 @@
 
 def kernel(
     n_line, n_tile, n_block, n_slot, n_shot,
-    traces, codes, routes, dip, table_hbm, beam_hbm, out,
-    tiles, halo, meta, table, beam, slots_v, slots, cosine, sine, stacked, part, r_main, r_top, r_bot,
+    traces_hbm, codes, routes, dip, table_hbm, beam_hbm, out,
+    traces, tiles, halo, meta, table, beam, slots_v, slots, cosine, sine, stacked, part, r_main, r_top, r_bot,
     local, main_send, main_recv, halo_send, halo_recv, head_send, head_recv, meta_send, meta_recv,
     part_send, part_recv, top_send, top_recv, bot_send, bot_recv,
 ):
@@ -51,6 +51,8 @@
     depth = n_slot * BR
     pieces = out.shape[1] * LANES // CW
 
+    own_fetch = pltpu.make_async_copy(traces_hbm, traces, local.at[6])
+    own_fetch.start()
     fetches = [pltpu.make_async_copy(table_hbm, table, local.at[0])]
     for i in range(4):
         rows = pl.ds(i * (2 * depth // 4), 2 * depth // 4)
@@ -77,6 +79,7 @@
         def _():
             greet(other, tile + 1)
 
+    own_fetch.wait()
     for i in range(n_full):
         tiles[tile, i] = jnp.transpose(traces[i * LANES : (i + 1) * LANES, :])
     meta[tile] = jnp.zeros((8, LANES), jnp.int32)
@@ -107,9 +110,15 @@
             device_id=(to_line, to_tile), device_id_type=MESH,
         )
 
-    def main_copy(source, way, to_tile):
-        block = tiles.at[source, pl.ds(0, n_full)]
-        return remote(block, block, main_send.at[source, way], main_recv.at[source], line, to_tile)
+    def main_piece(piece):
+        def main_copy(source, way, to_tile):
+            block = tiles.at[source, pl.ds(piece * (n_full // 2), n_full // 2)]
+            at = source * 2 + piece
+            return remote(block, block, main_send.at[at, way], main_recv.at[at], line, to_tile)
+
+        return main_copy
+
+    mains = [main_piece(0), main_piece(1)]
 
     def halo_copy(source, way, to_tile):
         block = halo.at[source]
@@ -124,25 +133,28 @@
         for k in range(1, n_tile)
     ]
 
-    def onward(copy, step, way, act):
+    distances = [(step, way) for step in range(1, n_z) for way in (1, -1)]
+
+    def along(copy, source, way, act):
+        @pl.when((z + way >= 0) & (z + way < n_z))
+        def _():
+            act(copy(source, 1 if way > 0 else 2, (z + way) * 2 + x))
+
+    def own(copy, act):
+        along(copy, tile, 1, act)
+        along(copy, tile, -1, act)
+        act(copy(tile, 0, across))
+
+    def onward(copy, step, way, act, arrive=False):
         come_from = z - step * way
         source = come_from * 2 + x
 
         @pl.when((come_from >= 0) & (come_from < n_z))
         def _():
-            if act == "start" and step:
+            if arrive:
                 copy(source, 0, across).wait_recv()
-            for slot, to in ((0, 1), (1, -1)):
-                if step and to != way:
-                    continue
-
-                @pl.when((z + to >= 0) & (z + to < n_z))
-                def _():
-                    c = copy(source, slot, (z + to) * 2 + x)
-                    c.start() if act == "start" else c.wait_send()
-
-            c = copy(source, 2, across)
-            c.start() if act == "start" else c.wait_send()
+            along(copy, source, way, act)
+            act(copy(source, 0, across))
 
     @pl.when(line > 0)
     def _():
@@ -150,13 +162,14 @@
 
     for c in meta_out:
         c.start()
-    onward(main_copy, 0, 1, "start")
+    for copy in mains:
+        own(copy, lambda c: c.start())
 
     @pl.when(line < n_line - 1)
     def _():
         head_out.wait_recv()
 
-    onward(halo_copy, 0, 1, "start")
+    own(halo_copy, lambda c: c.start())
 
     for k in range(1, n_tile):
         source = lax.rem(tile + k, n_tile)
@@ -179,32 +192,28 @@
             jnp.broadcast_to(rank[0:1], (n_slot, LANES)) == wanted, lane_slots + (f * n_block + 1), 0
         )
         before = before + jnp.sum(member[0:1], axis=1, keepdims=True)
-        angle = 2.0 * jnp.pi * row[1:2].astype(jnp.float32) / 256.0
-        upright = jnp.transpose(jnp.broadcast_to(angle, (LANES, LANES)))
-        sign = jnp.where(lax.broadcasted_iota(jnp.int32, (LANES, LANES), 0) < n_shot, 1.0, -1.0)
-        cosine[f] = upright
-        sine[f] = sign
     slots_v[...] = jnp.broadcast_to(jnp.sum(found, axis=1, keepdims=True), (n_slot, LANES))
     to_scalars = pltpu.make_async_copy(slots_v, slots, local.at[5])
     to_scalars.start()
 
-    for step in range(1, n_z):
-        for way in (1, -1):
-            onward(main_copy, step, way, "start")
-        for way in (1, -1):
-            onward(halo_copy, step, way, "start")
-
-    def phases(f, carry):
-        angle = cosine[f]
-        sine[f] = sine[f] * jnp.sin(angle)
-        cosine[f] = jnp.cos(angle)
-        return carry
-
-    lax.fori_loop(0, n_tile, phases, 0)
+    for step, way in distances:
+        for copy in mains:
+            onward(copy, step, way, lambda c: c.start(), True)
+    for step, way in distances:
+        onward(halo_copy, step, way, lambda c: c.start(), True)
+
+    code_rows = jnp.concatenate([meta[f, 1:2] for f in range(n_tile)], 0)
+    angle = 2.0 * jnp.pi * code_rows.astype(jnp.float32) / 256.0
+    sign = jnp.where(lax.broadcasted_iota(jnp.int32, angle.shape, 1) < n_shot, 1.0, -1.0)
+    for into, row in ((cosine, jnp.cos(angle)), (sine, jnp.sin(angle) * sign)):
+        columns = jnp.transpose(jnp.concatenate([row, jnp.zeros((LANES - n_tile, LANES), jnp.float32)], 0))
+        for f in range(n_tile):
+            into[f] = jnp.broadcast_to(columns[:, f : f + 1], (LANES, LANES))
 
     for place in range(n_z):
         source = place * 2 + 1 - x
-        main_copy(source, 0, across).wait_recv()
+        for copy in mains:
+            copy(source, 0, across).wait_recv()
         halo_copy(source, 0, across).wait_recv()
     for f in range(n_tile):
         rim = jnp.concatenate([halo[f], jnp.zeros((LANES - half, LANES), jnp.bfloat16)], 0)
@@ -236,7 +245,7 @@
         stacked[:, pl.ds(pl.multiple_of(at + depth, BR), BR)] = turned(beam_now).astype(jnp.bfloat16)
         return carry
 
-    lax.fori_loop(0, n_slot, one_slot, 0)
+    lax.fori_loop(0, n_slot, one_slot, 0, unroll=8)
 
     for fetch in fetches[1:]:
         fetch.wait()
@@ -290,11 +299,10 @@
 
     for c in meta_out:
         c.wait_send()
-    for copy in (main_copy, halo_copy):
-        onward(copy, 0, 1, "wait")
-        for step in range(1, n_z):
-            for way in (1, -1):
-                onward(copy, step, way, "wait")
+    for copy in (*mains, halo_copy):
+        own(copy, lambda c: c.wait_send())
+        for step, way in distances:
+            onward(copy, step, way, lambda c: c.wait_send())
 
     @pl.when(tile > 0)
     def _():
@@ -355,9 +363,10 @@
     result = pl.pallas_call(
         functools.partial(kernel, n_line, n_tile, n_block, n_slot, n_shot),
         out_shape=jax.ShapeDtypeStruct((rows, tall, LANES), f32),
-        in_specs=[vmem, vmem, vmem, pl.BlockSpec(memory_space=pltpu.SMEM), hbm, hbm],
+        in_specs=[hbm, vmem, vmem, pl.BlockSpec(memory_space=pltpu.SMEM), hbm, hbm],
         out_specs=vmem,
         scratch_shapes=[
+            pltpu.VMEM(traces.shape[1:], bf16),
             pltpu.VMEM((n_tile, n_full + 1, LANES, LANES), bf16),
             pltpu.VMEM((n_tile, WIN // 2, LANES), bf16),
             pltpu.VMEM((n_tile, 8, LANES), i32),
@@ -372,8 +381,8 @@
             pltpu.VMEM((n_line - 1, rows, pixels), bf16),
             pltpu.VMEM((n_line, rows, CW), bf16),
             pltpu.VMEM((n_line, rows, CW), bf16),
-            dma((6,)),
-            dma((n_tile, 3)), dma((n_tile,)),
+            dma((7,)),
+            dma((2 * n_tile, 3)), dma((2 * n_tile,)),
             dma((n_tile, 3)), dma((n_tile,)),
             dma, dma,
             dma((n_tile,)), dma((n_tile,)),
@@ -382,7 +391,7 @@
             dma((n_line,)), dma((n_line,)),
         ],
         compiler_params=pltpu.CompilerParams(
-            collective_id=0, has_side_effects=True, vmem_limit_bytes=50 * 2**20
+            collective_id=0, has_side_effects=True, vmem_limit_bytes=60 * 2**20
         ),
     )(traces[0], codes, routes, dip_filter, table, beam_matrix.reshape(2 * depth, pixels))
     return result.reshape(2, rows // 2, tall, LANES)

time: 44.7 us -> 37.1 us (0.83)
  Pallas kernels: 39.3 us -> 35.3 us
  local copies, waits for them, and re-layouts: 5.15 us -> 1.57 us
    pallas_call x1, Pallas kernels: 39.3 us -> 35.3 us  [per_device(): pl.pallas_call(functools.partial(kernel, n_line, n_tile, n_block, n_slot,...]
    unnamed x11 -> x1, local copies, waits for them, and re-layouts: 5.15 us -> 1.57 us
where the time goes in v3:
time: 37.1 us; the launch traced here: 36.9 us
  Pallas kernels  35.3 us (95%)
  local copies, waits for them, and re-layouts  1.57 us (4%)
    pallas_call x1, Pallas kernels, per_device(): pl.pallas_call(functools.partial(kernel, n_line, n_tile, n_block, n_slot,...  35.3 us
    unnamed x1, local copies, waits for them, and re-layouts  1.57 us

profile of v3, /device:TPU:0, one launch (start us, length us, event | category | flops | bytes accessed | tf_op | source)
XLA Modules:
  0.0 36.9 jit_solution(10588117811811603396)
XLA Ops:
  0.0 35.3 %shard_map.64 = f32[32,8,128]{2,1,0:T(8,128)} custom-call(bf16[512,128]{1,0:T(8,128)(2,1)} %bitcast.5, s32[1,64]{1,0:T(1,128)} %codes.1, s32[1,16]{1,0:T(1,128)} %routes.1, f32[5,5]{1,0:T(8,128)} %dip.1, bf16[32,256,128]{2,1,0:T(8,128)(2,1)} %constant.7.table_hbm, bf16[8192,1024]{1,0:T(8,128)(2,1)} %bitcast.3), custom_call_target="tpu_custom_call" | custom-call | tf_op jit(solution)/shard_map/pallas_call | solution.py:363
  35.4 1.6 %copy.8 = f32[2,16,8,128]{3,2,1,0:T(8,128)} copy(f32[2,16,8,128]{3,2,1,0:T(8,128)} %bitcast.4) | data formatting | bytes 262144
